TPU v7x, 32 devices: a whole 2x2x4 slice. The times are simulated.
32 devices in a mesh: dp: 4 (over x, core), ctx: 8 (over z, y).
Axes of the slice: x: 2, y: 2, z: 4, core: 2. Of those that a mesh axis runs over, the one named last changes fastest.
Arguments:
- queries: bfloat16 [4, 1024, 512], P('dp', 'ctx'), may hold values from -6 to 6
- keys: bfloat16 [4, 1024, 512], P('dp', 'ctx'), may hold values from -6 to 6
- values: bfloat16 [4, 1024, 512], P('dp', 'ctx'), may hold values from -6 to 6
- grad_out: bfloat16 [4, 1024, 8192], P('dp', 'ctx'), may hold values from -6 to 6
- out_weight: bfloat16 [512, 8192], P(None, 'ctx'), may hold values from -0.25 to 0.25
- residues: float32 [512, 16], P('ctx'), may hold values from -0.25 to 0.25
- decays: float32 [512, 16], P('ctx'), may hold values from 4.8828126e-05 to 0.1
Outputs:
- grad_queries: bfloat16 [4, 1024, 512], P('dp', None, 'ctx')
- grad_keys: bfloat16 [4, 1024, 512], P('dp', None, 'ctx')
- grad_values: bfloat16 [4, 1024, 512], P('dp', None, 'ctx')
- grad_weight: float32 [512, 8192], P(None, 'ctx')
- grad_residues: float32 [512, 16], P('ctx')
- grad_decays: float32 [512, 16], P('ctx')
All inputs are finite; a program needn't handle non-finite values.
Results may differ from a plain program's by a relative error of at most 0.017.
Values may be sent and summed in bfloat16 or wider, within the bound.
A program may use at most 128 MiB of HBM per device.

v0:
```python
import functools
import math

import jax
import jax.numpy as jnp
from jax import lax
from jax.experimental import pallas as pl
from jax.experimental.pallas import tpu as pltpu
from jax.sharding import PartitionSpec as P

FFT_COLS = 128


HIGHEST = lax.Precision.HIGHEST


def fourier_tables(fft_rows, fft_cols):
    total = fft_rows * fft_cols
    row_index = jnp.arange(fft_rows, dtype=jnp.int32)
    col_index = jnp.arange(fft_cols, dtype=jnp.int32)
    first = (row_index[:, None] * row_index[None, :] % fft_rows).astype(jnp.float32) * (
        2.0 * math.pi / fft_rows
    )
    twist = (row_index[:, None] * col_index[None, :] % total).astype(jnp.float32) * (
        2.0 * math.pi / total
    )
    second = (col_index[:, None] * col_index[None, :] % fft_cols).astype(jnp.float32) * (
        2.0 * math.pi / fft_cols
    )
    return (
        (jnp.cos(first), -jnp.sin(first)),
        (jnp.cos(twist), -jnp.sin(twist)),
        (jnp.cos(second), -jnp.sin(second)),
    )


def complex_product(left_re, left_im, right_re, right_im):
    return (left_re * right_re - left_im * right_im, left_re * right_im + left_im * right_re)


def apply_middle(table_re, table_im, data_re):

    def single(table, data):
        return jnp.einsum("kn,cnm->ckm", table, data, precision=HIGHEST)

    return (single(table_re, data_re), single(table_im, data_re))


def apply_last(table_re, table_im, data_re, data_im):

    def single(data, table):
        return jnp.einsum("ckm,mj->ckj", data, table, precision=HIGHEST)

    return (
        single(data_re, table_re) - single(data_im, table_im),
        single(data_im, table_re) + single(data_re, table_im),
    )


def forward_transform(signal, tables):
    (first_re, first_im), (twist_re, twist_im), (second_re, second_im) = tables
    section_re, section_im = apply_middle(first_re, first_im, signal)
    section_re, section_im = complex_product(section_re, section_im, twist_re, twist_im)
    return apply_last(second_re, second_im, section_re, section_im)


def inverse_transform(spec_re, spec_im, tables):
    (first_re, first_im), (twist_re, twist_im), (second_re, second_im) = tables
    section_re, section_im = apply_last(second_re, -second_im, spec_re, spec_im)
    section_re, section_im = complex_product(section_re, section_im, twist_re, -twist_im)
    result = jnp.einsum("kn,cnm->ckm", first_re, section_re, precision=HIGHEST) + jnp.einsum(
        "kn,cnm->ckm", first_im, section_im, precision=HIGHEST
    )
    total = first_re.shape[0] * second_re.shape[0]
    return result / float(total)


def padded_grid(signal, fft_rows, fft_cols):
    channels, seq_len = signal.shape
    padded = jnp.concatenate(
        [signal, jnp.zeros((channels, fft_rows * fft_cols - seq_len), jnp.float32)], axis=1
    )
    return padded.reshape(channels, fft_rows, fft_cols)


def leading_part(grid, seq_len):
    return grid.reshape(grid.shape[0], -1)[:, :seq_len]


def channels_first(block):
    return block[0].astype(jnp.float32).T


def rounded_sum(terms):
    rounded = lax.optimization_barrier(terms.astype(jnp.bfloat16))
    return jnp.sum(rounded.astype(jnp.float32), axis=0)


def body(queries, keys, values, grad_out, out_weight, residues, decays):
    channels = out_weight.shape[0]
    block_width = out_weight.shape[1]
    tok_rows = grad_out.shape[1]
    grad_cols = lax.all_to_all(grad_out, "ctx", split_axis=2, concat_axis=1, tiled=True)
    shard_piece = lax.all_gather(out_weight, "ctx", axis=1, tiled=True)
    blocks = shard_piece.shape[1] // block_width
    partial_value = grad_out[0]
    partial_value = partial_value.reshape(tok_rows, blocks, block_width)
    weight_part = shard_piece.reshape(channels, blocks, block_width)
    terms = jnp.einsum(
        "tks,cks->ktc", partial_value, weight_part, preferred_element_type=jnp.float32
    )
    gated_sum = rounded_sum(terms)
    grad_gated = gated_sum.astype(jnp.bfloat16)[None]
    query_ch, key_ch, value_ch, gated_grad_ch = (
        lax.all_to_all(queries, "ctx", split_axis=2, concat_axis=1, tiled=True),
        lax.all_to_all(keys, "ctx", split_axis=2, concat_axis=1, tiled=True),
        lax.all_to_all(values, "ctx", split_axis=2, concat_axis=1, tiled=True),
        lax.all_to_all(grad_gated, "ctx", split_axis=2, concat_axis=1, tiled=True),
    )
    grad_gated_full = channels_first(gated_grad_ch)
    seq_len = query_ch.shape[1]
    fft_rows = 2 * seq_len // FFT_COLS
    tables = fourier_tables(fft_rows, FFT_COLS)
    query_full = channels_first(query_ch)
    key_full = channels_first(key_ch)
    value_full = channels_first(value_ch)
    positions = jnp.arange(seq_len).astype(jnp.float32)
    decay_terms = jnp.exp(-decays[:, :, None] * positions[None, None, :])
    filter_taps = jnp.sum(residues[:, :, None] * decay_terms, axis=1)
    product = key_full * value_full
    grad_conv = grad_gated_full * query_full
    prod_re, prod_im = forward_transform(padded_grid(product, fft_rows, FFT_COLS), tables)
    taps_re, taps_im = forward_transform(padded_grid(filter_taps, fft_rows, FFT_COLS), tables)
    grad_re, grad_im = forward_transform(padded_grid(grad_conv, fft_rows, FFT_COLS), tables)
    conv_out = leading_part(
        inverse_transform(*complex_product(prod_re, prod_im, taps_re, taps_im), tables), seq_len
    )
    grad_product = leading_part(
        inverse_transform(*complex_product(taps_re, -taps_im, grad_re, grad_im), tables), seq_len
    )
    grad_taps = leading_part(
        inverse_transform(*complex_product(prod_re, -prod_im, grad_re, grad_im), tables), seq_len
    )
    gated = (query_full * conv_out).T.astype(jnp.bfloat16)[None]
    grad_queries = (grad_gated_full * conv_out).T.astype(jnp.bfloat16)[None]
    grad_keys = (grad_product * value_full).T.astype(jnp.bfloat16)[None]
    grad_values = (grad_product * key_full).T.astype(jnp.bfloat16)[None]
    partial_value = lax.dot_general(
        lax.all_gather(gated, "ctx", axis=2, tiled=True)[0],
        grad_cols[0],
        (((0,), (0,)), ((), ())),
        preferred_element_type=jnp.float32,
    )
    grad_weight = partial_value
    grad_residues = jnp.sum(grad_taps[:, None, :] * decay_terms, axis=2)
    grad_decays = -residues * jnp.sum(
        (grad_taps * positions[None, :])[:, None, :] * decay_terms, axis=2
    )
    grad_weight, grad_residues, grad_decays = (
        lax.psum(grad_weight.astype(jnp.bfloat16), "dp").astype(jnp.float32),
        lax.psum(grad_residues.astype(jnp.bfloat16), "dp").astype(jnp.float32),
        lax.psum(grad_decays.astype(jnp.bfloat16), "dp").astype(jnp.float32),
    )
    return (grad_queries, grad_keys, grad_values, grad_weight, grad_residues, grad_decays)

LANES = 128
MESH = pl.DeviceIdType.MESH
F32 = jnp.float32
BF16 = jnp.bfloat16


def dot_nt(left, right):
    return lax.dot_general(left, right, (((1,), (1,)), ((), ())), preferred_element_type=F32)


def split_rows(data):
    high = data.astype(BF16)
    low = (data - high.astype(F32)).astype(BF16)
    return jnp.concatenate([high, low], axis=0)


def fused_kernel(
    n_dp, n_ctx,
    q_ref, k_ref, v_ref, go_ref, w_ref, dec_ref, res_ref, res_plain_ref,
    gq_ref, gk_ref, gv_ref, dw_ref, par_ref,
    qkv_send, qkv_recv, gcols, wbuf, toep, etab, prod, conv, gconv, gprod,
    gat_send, gat_all, gg_acc, gg_send, gg_recv, ggt_send, ggt_recv,
    dwp, dwy, dwz, dwf, red, red_send, red_recv,
    q_ss, q_rs, g_ss, g_rs, w_ss, w_rs, a_ss, a_rs, b_ss, b_rs, c_ss, c_rs, t_ss, t_rs,
    y_ss, y_rs, z_ss, z_rs, f_ss, f_rs, r_ss, r_rs, loc_sem,
):
    me_d = lax.axis_index("dp")
    me_c = lax.axis_index("ctx")
    chans = q_ref.shape[2]
    mine = chans // n_ctx
    width = gcols.shape[2]
    block = width * n_dp
    order = dec_ref.shape[1]
    half = n_ctx // 2
    side = lax.rem(me_c, 2)
    partner = me_c + 1 - 2 * side
    ctx_peers = [lax.rem(me_c + s, n_ctx) for s in range(1, n_ctx)]
    dp_peers = [lax.rem(me_d + s, n_dp) for s in range(1, n_dp)]
    line_peers = [lax.rem(me_c + 2 * s, n_ctx) for s in range(1, half)]

    def remote(src, dst, ss, rs, **to):
        return pltpu.make_async_remote_copy(
            src_ref=src, dst_ref=dst, send_sem=ss, recv_sem=rs, device_id=to, device_id_type=MESH
        )

    def rows(index, size):
        return pl.ds(pl.multiple_of(index * size, size), size)

    barrier = pltpu.get_barrier_semaphore()
    for peer in ctx_peers:
        pl.semaphore_signal(barrier, inc=1, device_id={"ctx": peer}, device_id_type=MESH)
    for peer in dp_peers:
        pl.semaphore_signal(barrier, inc=1, device_id={"dp": peer}, device_id_type=MESH)

    for part, ref in enumerate((q_ref, k_ref, v_ref)):
        for at in range(0, chans, LANES):
            qkv_send[part, at : at + LANES, :] = ref[0, :, at : at + LANES].astype(F32).T.astype(BF16)
    pl.semaphore_wait(barrier, n_ctx - 1 + n_dp - 1)

    q_copies = [
        remote(qkv_send.at[:, rows(peer, mine), :], qkv_recv.at[me_c], q_ss.at[i], q_rs.at[i], ctx=peer)
        for i, peer in enumerate(ctx_peers)
    ]
    for copy in q_copies:
        copy.start()
    qkv_recv[me_c] = qkv_send[:, rows(me_c, mine), :]

    def cols_copy(i, peer, k):
        return remote(
            go_ref.at[0, :, rows(k * n_dp + peer, width)],
            gcols.at[k, rows(me_d, LANES), :],
            g_ss.at[i, k], g_rs.at[i, k], dp=peer,
        )

    def cols_own(k):
        return pltpu.make_async_copy(
            go_ref.at[0, :, rows(k * n_dp + me_d, width)], gcols.at[k, rows(me_d, LANES), :], loc_sem.at[k]
        )

    for k in range(n_ctx):
        for i, peer in enumerate(dp_peers):
            cols_copy(i, peer, k).start()
        cols_own(k).start()

    own_w = pltpu.make_async_copy(w_ref.at[:, rows(me_d, width)], wbuf.at[me_c], loc_sem.at[n_ctx])
    own_w.start()
    w_own = w_ref.at[:, rows(me_d, width)]
    w_copies = [
        remote(w_own, wbuf.at[me_c], w_ss.at[i], w_rs.at[i], ctx=peer)
        for i, peer in enumerate(line_peers + [partner])
    ]
    for copy in w_copies:
        copy.start()

    lane = lax.broadcasted_iota(jnp.int32, (order, LANES), 1).astype(F32)
    upper = lax.broadcasted_iota(jnp.int32, (LANES, LANES), 1) >= lax.broadcasted_iota(
        jnp.int32, (LANES, LANES), 0
    )
    block_row = lax.broadcasted_iota(jnp.int32, (n_ctx, LANES), 0)

    def tables(c, carry):
        rate = dec_ref[c]
        weight = res_ref[c]
        taps = []
        for m in range(n_ctx):
            at = lane + float(m * LANES)
            value = jnp.exp(-rate * at)
            timed = value * at
            etab[c, :, m * LANES : (m + 1) * LANES] = jnp.concatenate(
                [split_rows(value), split_rows(timed)], axis=0
            )
            taps.append(jnp.sum(weight * value, axis=0, keepdims=True))
        wide = jnp.broadcast_to(jnp.concatenate(taps, axis=1), (LANES, n_ctx * LANES))
        rolled = pltpu.roll(wide, 0, 1, stride=1, stride_axis=0)
        toep[c, :, 0:LANES] = jnp.where(upper, rolled[:, 0:LANES], 0.0).astype(BF16)
        toep[c, :, LANES:] = rolled[:, LANES:].astype(BF16)
        return carry

    lax.fori_loop(0, mine, tables, 0)

    for copy in q_copies:
        copy.wait()
    for j in range(n_ctx):
        prod[j * mine : (j + 1) * mine, :] = qkv_recv[j, 1].astype(F32) * qkv_recv[j, 2].astype(F32)

    def forward(c, carry):
        both = jnp.dot(split_rows(prod[pl.ds(c, n_ctx, stride=mine), :]), toep[c], preferred_element_type=F32)
        both = both[:n_ctx] + both[n_ctx:]
        total = both[:, 0:LANES]
        for m in range(1, n_ctx):
            moved = pltpu.roll(both[:, m * LANES : (m + 1) * LANES], m, 0)
            total = total + jnp.where(block_row >= m, moved, 0.0)
        conv[pl.ds(c, n_ctx, stride=mine), :] = total
        return carry

    lax.fori_loop(0, mine, forward, 0, unroll=4)

    for j in range(n_ctx):
        gat_send[j] = (qkv_recv[j, 0].astype(F32) * conv[j * mine : (j + 1) * mine, :]).astype(BF16)
    a_copies = [
        remote(
            gat_send.at[peer],
            gat_all.at[rows(me_c, mine), rows(me_d, LANES)],
            a_ss.at[i], a_rs.at[i], ctx=peer,
        )
        for i, peer in enumerate(ctx_peers)
    ]
    for copy in a_copies:
        copy.start()
    gat_all[rows(me_c, mine), rows(me_d, LANES)] = gat_send[me_c]

    forwards = []
    for i, peer in enumerate(line_peers):
        w_copies[i].wait()
        source = lax.rem(me_c + n_ctx - 2 * (i + 1), n_ctx)
        copy = remote(wbuf.at[source], wbuf.at[source], w_ss.at[half + i], w_rs.at[half + i], ctx=partner)
        copy.start()
        forwards.append(copy)

    for copy in a_copies:
        copy.wait()
    b_copies = [
        remote(
            gat_all.at[:, rows(me_d, LANES)], gat_all.at[:, rows(me_d, LANES)],
            b_ss.at[i], b_rs.at[i], dp=peer,
        )
        for i, peer in enumerate(dp_peers)
    ]
    for copy in b_copies:
        copy.start()

    for k in range(n_ctx):
        for i, peer in enumerate(dp_peers):
            cols_copy(i, peer, k).wait()
        cols_own(k).wait()
    own_w.wait()
    w_copies[half - 1].wait()
    for copy in forwards:
        copy.wait()

    gg_acc[...] = jnp.zeros_like(gg_acc)

    def terms(k, carry):
        gg_acc[...] += dot_nt(wbuf[k], gcols[k])
        return carry

    lax.fori_loop(0, n_ctx, terms, 0)
    gg_send[...] = gg_acc[...].astype(BF16)
    c_copies = [
        remote(gg_send.at[:, rows(peer, LANES)], gg_recv.at[me_d], c_ss.at[i], c_rs.at[i], dp=peer)
        for i, peer in enumerate(dp_peers)
    ]
    for copy in c_copies:
        copy.start()

    for copy in b_copies:
        copy.wait()

    def weight_block(k):
        return jnp.dot(gat_all[...], gcols[k], preferred_element_type=F32)

    y_copies = []
    for z in range(half):
        k = 2 * z + 1 - side
        dwp[k] = weight_block(k).astype(BF16)
        copy = remote(dwp.at[k], dwy.at[z], y_ss.at[z], y_rs.at[z], ctx=partner)
        copy.start()
        y_copies.append(copy)

    for copy in c_copies:
        copy.wait()
    gg_recv[me_d] = gg_send[:, rows(me_d, LANES)]
    total = gg_recv[0].astype(F32)
    for d in range(1, n_dp):
        total = total + gg_recv[d].astype(F32)
    ggt_send[...] = total.astype(BF16)
    t_copies = [
        remote(ggt_send.at[rows(peer, mine), :], ggt_recv.at[me_c], t_ss.at[i], t_rs.at[i], ctx=peer)
        for i, peer in enumerate(ctx_peers)
    ]
    for copy in t_copies:
        copy.start()
    ggt_recv[me_c] = ggt_send[rows(me_c, mine), :]

    def own_blocks(z, carry):
        k = 2 * z + side
        dwp[k] = weight_block(k).astype(BF16)
        return carry

    lax.fori_loop(0, half, own_blocks, 0)
    for copy in y_copies:
        copy.wait()
    z_copies = []
    for i, peer in enumerate(line_peers):
        dwp[peer] = (dwp[peer].astype(F32) + dwy[peer // 2].astype(F32)).astype(BF16)
        copy = remote(dwp.at[peer], dwz.at[i], z_ss.at[i], z_rs.at[i], ctx=peer)
        copy.start()
        z_copies.append(copy)

    for copy in t_copies:
        copy.wait()
    for j in range(n_ctx):
        part = slice(j * mine, (j + 1) * mine)
        gated_grad = ggt_recv[j].astype(F32)
        gconv[part, :] = gated_grad * qkv_recv[j, 0].astype(F32)
        gq_ref[j] = (gated_grad * conv[part, :]).astype(BF16)

    def window(c):
        grad = gconv[pl.ds(c, n_ctx, stride=mine), :]
        tiles = [grad]
        for m in range(1, n_ctx):
            moved = pltpu.roll(grad, n_ctx - m, 0)
            tiles.append(jnp.where(block_row < n_ctx - m, moved, 0.0))
        return jnp.concatenate(tiles, axis=1)

    def backward(c, carry):
        both = dot_nt(split_rows(window(c)), toep[c])
        gprod[pl.ds(c, n_ctx, stride=mine), :] = both[:n_ctx] + both[n_ctx:]
        return carry

    def lags(c, carry):
        left = prod[pl.ds(c, n_ctx, stride=mine), :].astype(BF16)
        outer = lax.dot_general(
            left, window(c).astype(BF16), (((0,), (0,)), ((), ())), preferred_element_type=F32
        )
        outer = jnp.concatenate(
            [jnp.where(upper, outer[:, 0:LANES], 0.0).astype(BF16), outer[:, LANES:].astype(BF16)], axis=1
        )
        sums = dot_nt(etab[c], outer)
        plain = sums[0:order] + sums[order : 2 * order]
        timed = sums[2 * order : 3 * order] + sums[3 * order :]
        grown = jnp.exp(dec_ref[c] * lane)
        red[c, 0:order, :] = plain * grown
        red[c, order:, :] = (timed - lane * plain) * grown
        return carry

    lax.fori_loop(0, mine, backward, 0, unroll=4)
    for copy in z_copies:
        copy.wait()
    last = dwp[me_c].astype(F32) + dwy[me_c // 2].astype(F32)
    for i in range(half - 1):
        last = last + dwz[i].astype(F32)
    dwf[:, rows(me_d, width)] = last.astype(BF16)
    f_copies = [
        remote(
            dwf.at[:, rows(me_d, width)], dwf.at[:, rows(me_d, width)], f_ss.at[i], f_rs.at[i], dp=peer
        )
        for i, peer in enumerate(dp_peers)
    ]
    for copy in f_copies:
        copy.start()

    lax.fori_loop(0, mine, lags, 0, unroll=2)
    sums = jnp.sum(red[...], axis=2)
    sums = jnp.concatenate([sums[:, :order], -res_plain_ref[...] * sums[:, order:]], axis=1)
    red_send[...] = jnp.concatenate([sums, jnp.zeros((mine, LANES - 2 * order), F32)], axis=1)
    r_copies = [
        remote(red_send, red_recv.at[me_d], r_ss.at[i], r_rs.at[i], dp=peer)
        for i, peer in enumerate(dp_peers)
    ]
    for copy in r_copies:
        copy.start()
    red_recv[me_d] = red_send[...]
    for j in range(n_ctx):
        part = slice(j * mine, (j + 1) * mine)
        gk_ref[j] = (gprod[part, :] * qkv_recv[j, 2].astype(F32)).astype(BF16)
        gv_ref[j] = (gprod[part, :] * qkv_recv[j, 1].astype(F32)).astype(BF16)
    for copy in f_copies:
        copy.wait()
    dw_ref[...] = dwf[...]
    for copy in r_copies:
        copy.wait()
    total = red_recv[0]
    for d in range(1, n_dp):
        total = total + red_recv[d]
    par_ref[...] = total


def fused_body(n_dp, n_ctx, queries, keys, values, grad_out, out_weight, residues, decays):
    chans, block = out_weight.shape
    mine, order = residues.shape
    width = block // n_dp
    wide = (mine, order, LANES)
    vm = pl.BlockSpec(memory_space=pltpu.VMEM)
    hbm = pl.BlockSpec(memory_space=pl.ANY)
    sem = pltpu.SemaphoreType.DMA
    n_c, n_d, half = n_ctx - 1, n_dp - 1, n_ctx // 2

    def twice(*shape):
        return [sem(shape), sem(shape)]

    scratch = [
        pltpu.VMEM((3, chans, LANES), BF16),
        pltpu.VMEM((n_ctx, 3, mine, LANES), BF16),
        pltpu.VMEM((n_ctx, n_dp * LANES, width), BF16),
        pltpu.VMEM((n_ctx, chans, width), BF16),
        pltpu.VMEM((mine, LANES, n_ctx * LANES), BF16),
        pltpu.VMEM((mine, 4 * order, n_ctx * LANES), BF16),
        pltpu.VMEM((chans, LANES), F32),
        pltpu.VMEM((chans, LANES), F32),
        pltpu.VMEM((chans, LANES), F32),
        pltpu.VMEM((chans, LANES), F32),
        pltpu.VMEM((n_ctx, mine, LANES), BF16),
        pltpu.VMEM((chans, n_dp * LANES), BF16),
        pltpu.VMEM((chans, n_dp * LANES), F32),
        pltpu.VMEM((chans, n_dp * LANES), BF16),
        pltpu.VMEM((n_dp, chans, LANES), BF16),
        pltpu.VMEM((chans, LANES), BF16),
        pltpu.VMEM((n_ctx, mine, LANES), BF16),
        pltpu.VMEM((n_ctx, chans, width), BF16),
        pltpu.VMEM((half, chans, width), BF16),
        pltpu.VMEM((half - 1, chans, width), BF16),
        pltpu.VMEM((chans, block), BF16),
        pltpu.VMEM((mine, 2 * order, LANES), F32),
        pltpu.VMEM((mine, LANES), F32),
        pltpu.VMEM((n_dp, mine, LANES), F32),
    ]
    scratch += twice(n_c) + twice(n_d, n_ctx) + twice(n_c) + twice(n_c) + twice(n_d) + twice(n_d)
    scratch += twice(n_c) + twice(half) + twice(half - 1) + twice(n_d) + twice(n_d) + [sem((n_ctx + 1,))]
    blocks = jax.ShapeDtypeStruct((n_ctx, mine, LANES), BF16)
    gq, gk, gv, dw, par = pl.pallas_call(
        functools.partial(fused_kernel, n_dp, n_ctx),
        out_shape=(
            blocks, blocks, blocks,
            jax.ShapeDtypeStruct((chans, block), BF16),
            jax.ShapeDtypeStruct((mine, LANES), F32),
        ),
        in_specs=[vm, vm, vm, hbm, hbm, vm, vm, vm],
        out_specs=(vm,) * 5,
        scratch_shapes=scratch,
        compiler_params=pltpu.CompilerParams(
            collective_id=0, has_side_effects=True, vmem_limit_bytes=58 * 1024 * 1024
        ),
        cost_estimate=pl.CostEstimate(flops=6 * 10**9, bytes_accessed=8 * 2**20, transcendentals=2**20),
    )(
        queries, keys, values, grad_out, out_weight,
        jnp.broadcast_to(decays[:, :, None], wide),
        jnp.broadcast_to(residues[:, :, None], wide),
        residues,
    )

    def positions_first(grid):
        return jnp.transpose(grid, (0, 2, 1)).reshape(1, n_ctx * LANES, mine)

    return (
        positions_first(gq), positions_first(gk), positions_first(gv),
        dw.astype(F32), par[:, :order], par[:, order : 2 * order],
    )


def fits_fused(n_dp, n_ctx, queries, grad_out, out_weight, residues):
    chans, columns = out_weight.shape
    return (
        n_ctx == 8
        and n_dp >= 2
        and queries.shape[0] == n_dp
        and queries.shape[1] == n_ctx * LANES
        and chans % (n_ctx * 16) == 0
        and chans % LANES == 0
        and columns % (n_ctx * n_dp * LANES) == 0
        and residues.shape[1] % 16 == 0
        and 2 * residues.shape[1] <= LANES
        and chans <= 512
        and columns <= 8192
    )


def solution(mesh):
    placed = (
        P("dp", "ctx", None),
        P("dp", "ctx", None),
        P("dp", "ctx", None),
        P("dp", "ctx", None),
        P(None, "ctx"),
        P("ctx", None),
        P("ctx", None),
    )
    n_dp, n_ctx = mesh.shape["dp"], mesh.shape["ctx"]

    outputs = (
        P("dp", None, "ctx"),
        P("dp", None, "ctx"),
        P("dp", None, "ctx"),
        P(None, "ctx"),
        P("ctx", None),
        P("ctx", None),
    )

    def run(queries, keys, values, grad_out, out_weight, residues, decays):
        inner = body
        if fits_fused(n_dp, n_ctx, queries, grad_out, out_weight, residues):
            inner = functools.partial(fused_body, n_dp, n_ctx)
        mapped = jax.shard_map(inner, mesh=mesh, in_specs=placed, out_specs=outputs, check_vma=False)
        return mapped(queries, keys, values, grad_out, out_weight, residues, decays)

    return run
```

profile of v0, /device:TPU:29, one launch (start us, length us, event | category | flops | bytes accessed | tf_op | source)
XLA Modules:
  0.0 138.4 jit_solution(4422279770941333872)
XLA Ops:
  0.6 0.8 copy.19.res_plain_ref
  1.4 0.0 copy-start.1
  1.4 0.8 copy.18
  2.2 1.0 broadcast_in_dim.4.dec_ref
  3.2 1.0 broadcast_in_dim.5.res_ref
  4.2 0.0 copy-done.1
  4.2 125.2 %shard_map.118 = (bf16[8,64,128]{2,1,0:T(8,128)(2,1)}, bf16[8,64,128]{2,1,0:T(8,128)(2,1)}, bf16[8,64,128]{2,1,0:T(8,128)(2,1)}, bf16[512,1024]{1,0:T(8,128)(2,1)}, f32[64,128]{1,0:T(8,128)}) custom-call(bf16[1,128,512]{2,1,0:T(8,128)(2,1)} %q_ref.1, bf16[1,128,512]{2,1,0:T(8,128)(2,1)} %k_ref.1, bf16[1,128,512]{2,1,0:T(8,128)(2,1)} %v_ref.1, ...), custom_call_target="tpu_custom_call" | custom-call | flops 6000000000 | bytes 8388608 | tf_op jit(solution)/shard_map/pallas_call | solution.py:526
  129.4 0.0 copy-start
  129.4 1.1 copy.21
  130.5 0.7 reshape.23
  131.2 1.0 copy.22
  132.2 0.7 reshape.24
  132.9 0.9 fusion
  133.8 0.7 copy.25
  134.5 0.7 copy.24
  135.1 1.0 copy.23
  136.1 0.7 reshape.25
  136.9 0.0 copy-done
  136.9 1.6 %convert_element_type.3 = f32[512,1024]{1,0:T(8,128)} convert(bf16[512,1024]{1,0:T(8,128)(2,1)S(1)} %copy-done) | non-fusion elementwise | flops 524288 | bytes 3145728 | tf_op jit(solution)/shard_map/convert_element_type | solution.py:552
Async XLA Ops:
  1.4 2.8 %copy-start.1 = (f32[64,16]{1,0:T(8,128)}, f32[64,16]{1,0:T(8,128)S(1)}, u32[]{:S(2)}) copy-start(f32[64,16]{1,0:T(8,128)S(1)} %copy.19.res_plain_ref) | copy-start | bytes 12292
  129.4 7.5 %copy-start = (bf16[512,1024]{1,0:T(8,128)(2,1)S(1)}, bf16[512,1024]{1,0:T(8,128)(2,1)}, u32[]{:S(2)}) copy-start(bf16[512,1024]{1,0:T(8,128)(2,1)} %get-tuple-element.14) | copy-start | bytes 3145732
where the time goes:
time: 139 us; the launch traced here: 138 us
  Pallas kernels  125 us (90%)
  local copies, waits for them, and re-layouts  11 us (8%)
  other arithmetic  1.57 us (1%)
    pallas_call x1, Pallas kernels, fused_body(): pl.pallas_call(functools.partial(fused_kernel, n_dp, n_ctx), out_shape=(b...  125 us
    transpose x3, local copies, waits for them, and re-layouts, positions_first(): return jnp.transpose(grid, (0, 2, 1)).reshape(1, n_ctx * LANES, mine)  3.07 us
    unnamed x8, local copies, waits for them, and re-layouts  2.92 us

commit v1 on v0

--- a/solution.py
+++ b/solution.py
@@ -181,9 +181,10 @@
 
 def fused_kernel(
     n_dp, n_ctx,
-    q_ref, k_ref, v_ref, go_ref, w_ref, dec_ref, res_ref, res_plain_ref,
-    gq_ref, gk_ref, gv_ref, dw_ref, par_ref,
-    qkv_send, qkv_recv, gcols, wbuf, toep, etab, prod, conv, gconv, gprod,
+    q_ref, k_ref, v_ref, go_ref, w_ref, dec_ref, res_ref,
+    gq_ref, gk_ref, gv_ref, dw_ref, par_res_ref, par_dec_ref,
+    qkv_send, qkv_recv, gcols, wbuf, toep, etab, utab, vtab, cmat, bmat, dec_wide, res_wide,
+    prod, conv, gconv, gprod, ubuf, sbuf, vbuf, zbuf,
     gat_send, gat_all, gg_acc, gg_send, gg_recv, ggt_send, ggt_recv,
     dwp, dwy, dwz, dwf, red, red_send, red_recv,
     q_ss, q_rs, g_ss, g_rs, w_ss, w_rs, a_ss, a_rs, b_ss, b_rs, c_ss, c_rs, t_ss, t_rs,
@@ -194,8 +195,8 @@
     chans = q_ref.shape[2]
     mine = chans // n_ctx
     width = gcols.shape[2]
-    block = width * n_dp
-    order = dec_ref.shape[1]
+    order = dec_ref.shape[0]
+    block_rows = chans // 2
     half = n_ctx // 2
     side = lax.rem(me_c, 2)
     partner = me_c + 1 - 2 * side
@@ -261,44 +262,65 @@
     upper = lax.broadcasted_iota(jnp.int32, (LANES, LANES), 1) >= lax.broadcasted_iota(
         jnp.int32, (LANES, LANES), 0
     )
-    block_row = lax.broadcasted_iota(jnp.int32, (n_ctx, LANES), 0)
+    column = lax.broadcasted_iota(jnp.int32, (mine, LANES), 1)
+    rates, weights = dec_ref[...], res_ref[...]
+    for c in range(mine):
+        dec_wide[c] = jnp.broadcast_to(rates[:, c : c + 1], (order, LANES))
+        res_wide[c] = jnp.broadcast_to(weights[:, c : c + 1], (order, LANES))
+    rate_rows, weight_rows = rates.T, weights.T
+    rest = jnp.zeros((mine, LANES - 2 * order), F32)
+    fade = jnp.exp(-float(LANES) * jnp.concatenate([rate_rows, rate_rows, rest], axis=1))
+    step = jnp.where((column >= order) & (column < 2 * order), float(LANES), 0.0)
+    weight_rows = jnp.concatenate([weight_rows, jnp.zeros((mine, LANES - order), F32)], axis=1)
+    blank = jnp.zeros((LANES - 2 * order, LANES), F32)
 
     def tables(c, carry):
-        rate = dec_ref[c]
-        weight = res_ref[c]
-        taps = []
-        for m in range(n_ctx):
-            at = lane + float(m * LANES)
-            value = jnp.exp(-rate * at)
-            timed = value * at
-            etab[c, :, m * LANES : (m + 1) * LANES] = jnp.concatenate(
-                [split_rows(value), split_rows(timed)], axis=0
-            )
-            taps.append(jnp.sum(weight * value, axis=0, keepdims=True))
-        wide = jnp.broadcast_to(jnp.concatenate(taps, axis=1), (LANES, n_ctx * LANES))
-        rolled = pltpu.roll(wide, 0, 1, stride=1, stride_axis=0)
-        toep[c, :, 0:LANES] = jnp.where(upper, rolled[:, 0:LANES], 0.0).astype(BF16)
-        toep[c, :, LANES:] = rolled[:, LANES:].astype(BF16)
-        return carry
-
-    lax.fori_loop(0, mine, tables, 0)
+        rate = dec_wide[c]
+        weight = res_wide[c]
+        value = jnp.exp(-rate * lane)
+        etab[c] = jnp.concatenate([split_rows(value), split_rows(value * lane)], axis=0)
+        after = jnp.exp(-rate * (lane + 1.0))
+        before = jnp.exp(-rate * (LANES - 1.0 - lane))
+        cmat[c] = (weight * after).astype(BF16)
+        bmat[c] = before.astype(BF16)
+        vtab[c] = jnp.concatenate([after, after * (lane + 1.0), blank], axis=0).astype(BF16)
+        utab[c] = jnp.concatenate([before, before * (LANES - 1.0 - lane), blank], axis=0).astype(BF16)
+        taps = jnp.sum(weight * value, axis=0, keepdims=True)
+        rolled = pltpu.roll(jnp.broadcast_to(taps, (LANES, LANES)), 0, 1, stride=1, stride_axis=0)
+        toep[c] = jnp.where(upper, rolled, 0.0).astype(BF16)
+        return carry
+
+    lax.fori_loop(0, mine, tables, 0, unroll=4)
+
+    def channel(ref, c):
+        return ref[pl.ds(c, n_ctx, stride=mine), :]
+
+    def joined(both):
+        return both[:n_ctx] + both[n_ctx:]
 
     for copy in q_copies:
         copy.wait()
     for j in range(n_ctx):
         prod[j * mine : (j + 1) * mine, :] = qkv_recv[j, 1].astype(F32) * qkv_recv[j, 2].astype(F32)
 
+    def enter(c, carry):
+        ubuf[pl.ds(c, n_ctx, stride=mine), :] = joined(dot_nt(split_rows(channel(prod, c)), utab[c]))
+        return carry
+
+    lax.fori_loop(0, mine, enter, 0, unroll=8)
+    state = jnp.zeros((mine, LANES), F32)
+    for j in range(n_ctx):
+        part = slice(j * mine, (j + 1) * mine)
+        sbuf[part, :] = state
+        state = fade * (state + step * pltpu.roll(state, order, 1)) + ubuf[part, :]
+
     def forward(c, carry):
-        both = jnp.dot(split_rows(prod[pl.ds(c, n_ctx, stride=mine), :]), toep[c], preferred_element_type=F32)
-        both = both[:n_ctx] + both[n_ctx:]
-        total = both[:, 0:LANES]
-        for m in range(1, n_ctx):
-            moved = pltpu.roll(both[:, m * LANES : (m + 1) * LANES], m, 0)
-            total = total + jnp.where(block_row >= m, moved, 0.0)
-        conv[pl.ds(c, n_ctx, stride=mine), :] = total
-        return carry
-
-    lax.fori_loop(0, mine, forward, 0, unroll=4)
+        near = jnp.dot(split_rows(channel(prod, c)), toep[c], preferred_element_type=F32)
+        far = jnp.dot(split_rows(channel(sbuf, c))[:, :order], cmat[c], preferred_element_type=F32)
+        conv[pl.ds(c, n_ctx, stride=mine), :] = joined(near + far)
+        return carry
+
+    lax.fori_loop(0, mine, forward, 0, unroll=8)
 
     for j in range(n_ctx):
         gat_send[j] = (qkv_recv[j, 0].astype(F32) * conv[j * mine : (j + 1) * mine, :]).astype(BF16)
@@ -314,14 +336,6 @@
         copy.start()
     gat_all[rows(me_c, mine), rows(me_d, LANES)] = gat_send[me_c]
 
-    forwards = []
-    for i, peer in enumerate(line_peers):
-        w_copies[i].wait()
-        source = lax.rem(me_c + n_ctx - 2 * (i + 1), n_ctx)
-        copy = remote(wbuf.at[source], wbuf.at[source], w_ss.at[half + i], w_rs.at[half + i], ctx=partner)
-        copy.start()
-        forwards.append(copy)
-
     for copy in a_copies:
         copy.wait()
     b_copies = [
@@ -334,20 +348,89 @@
     for copy in b_copies:
         copy.start()
 
+    forwards = []
+    for i, peer in enumerate(line_peers):
+        w_copies[i].wait()
+        source = lax.rem(me_c + n_ctx - 2 * (i + 1), n_ctx)
+        copy = remote(wbuf.at[source], wbuf.at[source], w_ss.at[half + i], w_rs.at[half + i], ctx=partner)
+        copy.start()
+        forwards.append(copy)
+
+    for copy in b_copies:
+        copy.wait()
     for k in range(n_ctx):
         for i, peer in enumerate(dp_peers):
             cols_copy(i, peer, k).wait()
         cols_own(k).wait()
+
+    def weight_block(k, h):
+        part = slice(h * block_rows, (h + 1) * block_rows)
+        dwp[k, part, :] = jnp.dot(gat_all[part, :], gcols[k], preferred_element_type=F32).astype(BF16)
+
+    def part_of(h):
+        return slice(h * block_rows, (h + 1) * block_rows)
+
+    line = me_c // 2
+    y_copies = {}
+    for h in range(2):
+        for s in list(range(1, half)) + [0]:
+            k = 2 * lax.rem(line + s, half) + 1 - side
+            weight_block(k, h)
+            copy = remote(
+                dwp.at[k, part_of(h), :], dwy.at[s, part_of(h), :], y_ss.at[h, s], y_rs.at[h, s], ctx=partner
+            )
+            copy.start()
+            y_copies[h, s] = copy
+
+    def own_blocks(z, carry):
+        for h in range(2):
+            weight_block(2 * z + side, h)
+        return carry
+
+    lax.fori_loop(0, half, own_blocks, 0)
+
     own_w.wait()
     w_copies[half - 1].wait()
     for copy in forwards:
         copy.wait()
-
     gg_acc[...] = jnp.zeros_like(gg_acc)
 
     def terms(k, carry):
         gg_acc[...] += dot_nt(wbuf[k], gcols[k])
         return carry
+
+    z_copies = {}
+
+    def pass_on(h):
+        part = part_of(h)
+        for i, peer in enumerate(line_peers):
+            y_copies[h, i + 1].wait()
+            dwp[peer, part, :] = (dwp[peer, part, :].astype(F32) + dwy[i + 1, part, :].astype(F32)).astype(BF16)
+            copy = remote(
+                dwp.at[peer, part, :], dwz.at[i, part, :], z_ss.at[h, i], z_rs.at[h, i], ctx=peer
+            )
+            copy.start()
+            z_copies[h, i] = copy
+
+    def finish(h):
+        part = part_of(h)
+        for i in range(half - 1):
+            z_copies[h, i].wait()
+        y_copies[h, 0].wait()
+        last = dwp[me_c, part, :].astype(F32) + dwy[0, part, :].astype(F32)
+        for i in range(half - 1):
+            last = last + dwz[i, part, :].astype(F32)
+        dwf[part, rows(me_d, width)] = last.astype(BF16)
+        copies = [
+            remote(
+                dwf.at[part, rows(me_d, width)], dwf.at[part, rows(me_d, width)],
+                f_ss.at[h, i], f_rs.at[h, i], dp=peer,
+            )
+            for i, peer in enumerate(dp_peers)
+        ]
+        for copy in copies:
+            copy.start()
+        return copies
 
     lax.fori_loop(0, n_ctx, terms, 0)
     gg_send[...] = gg_acc[...].astype(BF16)
@@ -357,24 +440,11 @@
     ]
     for copy in c_copies:
         copy.start()
-
-    for copy in b_copies:
-        copy.wait()
-
-    def weight_block(k):
-        return jnp.dot(gat_all[...], gcols[k], preferred_element_type=F32)
-
-    y_copies = []
-    for z in range(half):
-        k = 2 * z + 1 - side
-        dwp[k] = weight_block(k).astype(BF16)
-        copy = remote(dwp.at[k], dwy.at[z], y_ss.at[z], y_rs.at[z], ctx=partner)
-        copy.start()
-        y_copies.append(copy)
+    gg_recv[me_d] = gg_send[:, rows(me_d, LANES)]
+    pass_on(0)
 
     for copy in c_copies:
         copy.wait()
-    gg_recv[me_d] = gg_send[:, rows(me_d, LANES)]
     total = gg_recv[0].astype(F32)
     for d in range(1, n_dp):
         total = total + gg_recv[d].astype(F32)
@@ -386,21 +456,7 @@
     for copy in t_copies:
         copy.start()
     ggt_recv[me_c] = ggt_send[rows(me_c, mine), :]
-
-    def own_blocks(z, carry):
-        k = 2 * z + side
-        dwp[k] = weight_block(k).astype(BF16)
-        return carry
-
-    lax.fori_loop(0, half, own_blocks, 0)
-    for copy in y_copies:
-        copy.wait()
-    z_copies = []
-    for i, peer in enumerate(line_peers):
-        dwp[peer] = (dwp[peer].astype(F32) + dwy[peer // 2].astype(F32)).astype(BF16)
-        copy = remote(dwp.at[peer], dwz.at[i], z_ss.at[i], z_rs.at[i], ctx=peer)
-        copy.start()
-        z_copies.append(copy)
+    pass_on(1)
 
     for copy in t_copies:
         copy.wait()
@@ -408,57 +464,48 @@
         part = slice(j * mine, (j + 1) * mine)
         gated_grad = ggt_recv[j].astype(F32)
         gconv[part, :] = gated_grad * qkv_recv[j, 0].astype(F32)
-        gq_ref[j] = (gated_grad * conv[part, :]).astype(BF16)
-
-    def window(c):
-        grad = gconv[pl.ds(c, n_ctx, stride=mine), :]
-        tiles = [grad]
-        for m in range(1, n_ctx):
-            moved = pltpu.roll(grad, n_ctx - m, 0)
-            tiles.append(jnp.where(block_row < n_ctx - m, moved, 0.0))
-        return jnp.concatenate(tiles, axis=1)
+        gq_ref[:, j * LANES : (j + 1) * LANES] = (gated_grad * conv[part, :]).astype(BF16)
+
+    def leave(c, carry):
+        vbuf[pl.ds(c, n_ctx, stride=mine), :] = joined(dot_nt(split_rows(channel(gconv, c)), vtab[c]))
+        return carry
+
+    lax.fori_loop(0, mine, leave, 0, unroll=8)
+    state = jnp.zeros((mine, LANES), F32)
+    plain_sum, timed_sum = state, state
+    for j in reversed(range(n_ctx)):
+        part = slice(j * mine, (j + 1) * mine)
+        zbuf[part, :] = state
+        left, right = vbuf[part, :], sbuf[part, :]
+        state = fade * state + weight_rows * left
+        plain_sum = plain_sum + left * right
+        timed_sum = timed_sum + left * pltpu.roll(right, order, 1) + pltpu.roll(left, order, 1) * right
+    far_sums = jnp.where(column < order, plain_sum, jnp.where(column < 2 * order, timed_sum, 0.0))
 
     def backward(c, carry):
-        both = dot_nt(split_rows(window(c)), toep[c])
-        gprod[pl.ds(c, n_ctx, stride=mine), :] = both[:n_ctx] + both[n_ctx:]
+        near = dot_nt(split_rows(channel(gconv, c)), toep[c])
+        far = jnp.dot(split_rows(channel(zbuf, c))[:, :order], bmat[c], preferred_element_type=F32)
+        gprod[pl.ds(c, n_ctx, stride=mine), :] = joined(near + far)
         return carry
 
     def lags(c, carry):
-        left = prod[pl.ds(c, n_ctx, stride=mine), :].astype(BF16)
         outer = lax.dot_general(
-            left, window(c).astype(BF16), (((0,), (0,)), ((), ())), preferred_element_type=F32
+            channel(prod, c).astype(BF16), channel(gconv, c).astype(BF16),
+            (((0,), (0,)), ((), ())), preferred_element_type=F32,
         )
-        outer = jnp.concatenate(
-            [jnp.where(upper, outer[:, 0:LANES], 0.0).astype(BF16), outer[:, LANES:].astype(BF16)], axis=1
-        )
-        sums = dot_nt(etab[c], outer)
+        sums = dot_nt(etab[c], jnp.where(upper, outer, 0.0).astype(BF16))
         plain = sums[0:order] + sums[order : 2 * order]
         timed = sums[2 * order : 3 * order] + sums[3 * order :]
-        grown = jnp.exp(dec_ref[c] * lane)
+        grown = jnp.exp(dec_wide[c] * lane)
         red[c, 0:order, :] = plain * grown
         red[c, order:, :] = (timed - lane * plain) * grown
         return carry
 
-    lax.fori_loop(0, mine, backward, 0, unroll=4)
-    for copy in z_copies:
-        copy.wait()
-    last = dwp[me_c].astype(F32) + dwy[me_c // 2].astype(F32)
-    for i in range(half - 1):
-        last = last + dwz[i].astype(F32)
-    dwf[:, rows(me_d, width)] = last.astype(BF16)
-    f_copies = [
-        remote(
-            dwf.at[:, rows(me_d, width)], dwf.at[:, rows(me_d, width)], f_ss.at[i], f_rs.at[i], dp=peer
-        )
-        for i, peer in enumerate(dp_peers)
-    ]
-    for copy in f_copies:
-        copy.start()
-
-    lax.fori_loop(0, mine, lags, 0, unroll=2)
+    lax.fori_loop(0, mine, lags, 0, unroll=4)
+    f_copies = finish(0)
     sums = jnp.sum(red[...], axis=2)
-    sums = jnp.concatenate([sums[:, :order], -res_plain_ref[...] * sums[:, order:]], axis=1)
-    red_send[...] = jnp.concatenate([sums, jnp.zeros((mine, LANES - 2 * order), F32)], axis=1)
+    sums = jnp.concatenate([sums, rest], axis=1) + far_sums
+    red_send[...] = jnp.where(column < order, sums, -pltpu.roll(weight_rows, order, 1) * sums)
     r_copies = [
         remote(red_send, red_recv.at[me_d], r_ss.at[i], r_rs.at[i], dp=peer)
         for i, peer in enumerate(dp_peers)
@@ -466,26 +513,30 @@
     for copy in r_copies:
         copy.start()
     red_recv[me_d] = red_send[...]
+    lax.fori_loop(0, mine, backward, 0, unroll=8)
+    f_copies += finish(1)
     for j in range(n_ctx):
         part = slice(j * mine, (j + 1) * mine)
-        gk_ref[j] = (gprod[part, :] * qkv_recv[j, 2].astype(F32)).astype(BF16)
-        gv_ref[j] = (gprod[part, :] * qkv_recv[j, 1].astype(F32)).astype(BF16)
-    for copy in f_copies:
-        copy.wait()
-    dw_ref[...] = dwf[...]
+        at = slice(j * LANES, (j + 1) * LANES)
+        gk_ref[:, at] = (gprod[part, :] * qkv_recv[j, 2].astype(F32)).astype(BF16)
+        gv_ref[:, at] = (gprod[part, :] * qkv_recv[j, 1].astype(F32)).astype(BF16)
     for copy in r_copies:
         copy.wait()
     total = red_recv[0]
     for d in range(1, n_dp):
         total = total + red_recv[d]
-    par_ref[...] = total
+    turned = total.T
+    par_res_ref[...] = turned[0:order, :]
+    par_dec_ref[...] = turned[order : 2 * order, :]
+    for copy in f_copies:
+        copy.wait()
+    dw_ref[...] = dwf[...]
 
 
 def fused_body(n_dp, n_ctx, queries, keys, values, grad_out, out_weight, residues, decays):
     chans, block = out_weight.shape
     mine, order = residues.shape
     width = block // n_dp
-    wide = (mine, order, LANES)
     vm = pl.BlockSpec(memory_space=pltpu.VMEM)
     hbm = pl.BlockSpec(memory_space=pl.ANY)
     sem = pltpu.SemaphoreType.DMA
@@ -499,8 +550,18 @@
         pltpu.VMEM((n_ctx, 3, mine, LANES), BF16),
         pltpu.VMEM((n_ctx, n_dp * LANES, width), BF16),
         pltpu.VMEM((n_ctx, chans, width), BF16),
-        pltpu.VMEM((mine, LANES, n_ctx * LANES), BF16),
-        pltpu.VMEM((mine, 4 * order, n_ctx * LANES), BF16),
+        pltpu.VMEM((mine, LANES, LANES), BF16),
+        pltpu.VMEM((mine, 4 * order, LANES), BF16),
+        pltpu.VMEM((mine, LANES, LANES), BF16),
+        pltpu.VMEM((mine, LANES, LANES), BF16),
+        pltpu.VMEM((mine, order, LANES), BF16),
+        pltpu.VMEM((mine, order, LANES), BF16),
+        pltpu.VMEM((mine, order, LANES), F32),
+        pltpu.VMEM((mine, order, LANES), F32),
+        pltpu.VMEM((chans, LANES), F32),
+        pltpu.VMEM((chans, LANES), F32),
+        pltpu.VMEM((chans, LANES), F32),
+        pltpu.VMEM((chans, LANES), F32),
         pltpu.VMEM((chans, LANES), F32),
         pltpu.VMEM((chans, LANES), F32),
         pltpu.VMEM((chans, LANES), F32),
@@ -521,17 +582,18 @@
         pltpu.VMEM((n_dp, mine, LANES), F32),
     ]
     scratch += twice(n_c) + twice(n_d, n_ctx) + twice(n_c) + twice(n_c) + twice(n_d) + twice(n_d)
-    scratch += twice(n_c) + twice(half) + twice(half - 1) + twice(n_d) + twice(n_d) + [sem((n_ctx + 1,))]
-    blocks = jax.ShapeDtypeStruct((n_ctx, mine, LANES), BF16)
-    gq, gk, gv, dw, par = pl.pallas_call(
+    scratch += twice(n_c) + twice(2, half) + twice(2, half - 1) + twice(2, n_d) + twice(n_d) + [sem((n_ctx + 1,))]
+    blocks = jax.ShapeDtypeStruct((mine, n_ctx * LANES), BF16)
+    params = jax.ShapeDtypeStruct((order, mine), F32)
+    gq, gk, gv, dw, par_res, par_dec = pl.pallas_call(
         functools.partial(fused_kernel, n_dp, n_ctx),
         out_shape=(
             blocks, blocks, blocks,
             jax.ShapeDtypeStruct((chans, block), BF16),
-            jax.ShapeDtypeStruct((mine, LANES), F32),
+            params, params,
         ),
-        in_specs=[vm, vm, vm, hbm, hbm, vm, vm, vm],
-        out_specs=(vm,) * 5,
+        in_specs=[vm, vm, vm, hbm, hbm, vm, vm],
+        out_specs=(vm,) * 6,
         scratch_shapes=scratch,
         compiler_params=pltpu.CompilerParams(
             collective_id=0, has_side_effects=True, vmem_limit_bytes=58 * 1024 * 1024
@@ -539,17 +601,15 @@
         cost_estimate=pl.CostEstimate(flops=6 * 10**9, bytes_accessed=8 * 2**20, transcendentals=2**20),
     )(
         queries, keys, values, grad_out, out_weight,
-        jnp.broadcast_to(decays[:, :, None], wide),
-        jnp.broadcast_to(residues[:, :, None], wide),
-        residues,
+        decays.T, residues.T,
     )
 
     def positions_first(grid):
-        return jnp.transpose(grid, (0, 2, 1)).reshape(1, n_ctx * LANES, mine)
+        return grid.T[None]
 
     return (
         positions_first(gq), positions_first(gk), positions_first(gv),
-        dw.astype(F32), par[:, :order], par[:, order : 2 * order],
+        dw.astype(F32), par_res.T, par_dec.T,
     )
 
 

time: 139 us -> 118 us (0.85)
  the two profiles are of different devices: /device:TPU:29 before, /device:TPU:0 now
where the time goes in v1:
time: 118 us; the launch traced here: 117 us
  Pallas kernels  110 us (93%)
  local copies, waits for them, and re-layouts  3.18 us (3%)
  other arithmetic  2.86 us (2%)
    pallas_call x1, Pallas kernels, fused_body(): pl.pallas_call(functools.partial(fused_kernel, n_dp, n_ctx), out_shape=(b...  110 us
    unnamed x15, local copies, waits for them, and re-layouts  3.18 us
    convert_element_type x1, other arithmetic, fused_body(): dw.astype(F32)  2.86 us

profile of v1, /device:TPU:0, one launch (start us, length us, event | category | flops | bytes accessed | tf_op | source)
XLA Modules:
  0.0 117.2 jit_solution(4272648757480325094)
XLA Ops:
  0.6 110.5 %shard_map.118 = (bf16[64,1024]{1,0:T(8,128)(2,1)}, bf16[64,1024]{1,0:T(8,128)(2,1)}, bf16[64,1024]{1,0:T(8,128)(2,1)}, bf16[512,1024]{1,0:T(8,128)(2,1)}, f32[16,64]{1,0:T(8,128)}, /*index=5*/f32[16,64]{1,0:T(8,128)}) custom-call(bf16[1,128,512]{2,1,0:T(8,128)(2,1)} %q_ref.1, bf16[1,128,512]{2,1,0:T(8,128)(2,1)} %k_ref.1, bf16[1,128,512]{2,1,0:T(8,128)(2,1)} %v_ref.1, ...), custom_call_target="tpu_custom_call" | custom-call | flops 6000000000 | bytes 8388608 | tf_op jit(solution)/shard_map/pallas_call | solution.py:588
  111.1 0.0 copy-start.2
  111.1 0.0 copy-start.1
  111.1 0.0 copy-start
  111.1 0.0 copy-start.4
  111.1 0.0 copy-start.3
  111.2 2.9 %convert_element_type.3 = f32[512,1024]{1,0:T(8,128)} convert(bf16[512,1024]{1,0:T(8,128)(2,1)} %get-tuple-element.15) | non-fusion elementwise | flops 524288 | bytes 3145728 | tf_op jit(solution)/shard_map/convert_element_type | solution.py:612
  114.0 0.0 copy-done.2
  114.0 0.7 copy.18
  114.7 0.0 copy-done.1
  114.7 0.7 copy.19
  115.3 0.0 copy-done
  115.3 0.7 copy.20
  116.0 0.0 copy-done.4
  116.0 0.6 copy.21
  116.6 0.0 copy-done.3
  116.6 0.6 copy.22
Async XLA Ops:
  111.1 2.9 %copy-start.2 = (bf16[64,1024]{1,0:T(8,128)(2,1)S(1)}, bf16[64,1024]{1,0:T(8,128)(2,1)}, u32[]{:S(2)}) copy-start(bf16[64,1024]{1,0:T(8,128)(2,1)} %get-tuple-element.12) | copy-start | bytes 393220
  111.1 3.6 %copy-start.1 = (bf16[64,1024]{1,0:T(8,128)(2,1)S(1)}, bf16[64,1024]{1,0:T(8,128)(2,1)}, u32[]{:S(2)}) copy-start(bf16[64,1024]{1,0:T(8,128)(2,1)} %get-tuple-element.13) | copy-start | bytes 393220
  111.1 4.2 %copy-start = (bf16[64,1024]{1,0:T(8,128)(2,1)S(1)}, bf16[64,1024]{1,0:T(8,128)(2,1)}, u32[]{:S(2)}) copy-start(bf16[64,1024]{1,0:T(8,128)(2,1)} %get-tuple-element.14) | copy-start | bytes 393220
  111.1 4.9 %copy-start.4 = (f32[16,64]{1,0:T(8,128)S(1)}, f32[16,64]{1,0:T(8,128)}, u32[]{:S(2)}) copy-start(f32[16,64]{1,0:T(8,128)} %get-tuple-element.16) | copy-start | bytes 12292
  111.1 5.4 %copy-start.3 = (f32[16,64]{1,0:T(8,128)S(1)}, f32[16,64]{1,0:T(8,128)}, u32[]{:S(2)}) copy-start(f32[16,64]{1,0:T(8,128)} %get-tuple-element.17) | copy-start | bytes 12292

commit v2 on v1

--- a/solution.py
+++ b/solution.py
@@ -164,6 +164,7 @@
     return (grad_queries, grad_keys, grad_values, grad_weight, grad_residues, grad_decays)
 
 LANES = 128
+PARTS = 4
 MESH = pl.DeviceIdType.MESH
 F32 = jnp.float32
 BF16 = jnp.bfloat16
@@ -196,7 +197,7 @@
     mine = chans // n_ctx
     width = gcols.shape[2]
     order = dec_ref.shape[0]
-    block_rows = chans // 2
+    block_rows = chans // PARTS
     half = n_ctx // 2
     side = lax.rem(me_c, 2)
     partner = me_c + 1 - 2 * side
@@ -255,8 +256,7 @@
         remote(w_own, wbuf.at[me_c], w_ss.at[i], w_rs.at[i], ctx=peer)
         for i, peer in enumerate(line_peers + [partner])
     ]
-    for copy in w_copies:
-        copy.start()
+    w_copies[half - 1].start()
 
     lane = lax.broadcasted_iota(jnp.int32, (order, LANES), 1).astype(F32)
     upper = lax.broadcasted_iota(jnp.int32, (LANES, LANES), 1) >= lax.broadcasted_iota(
@@ -300,6 +300,8 @@
 
     for copy in q_copies:
         copy.wait()
+    for copy in w_copies[: half - 1]:
+        copy.start()
     for j in range(n_ctx):
         prod[j * mine : (j + 1) * mine, :] = qkv_recv[j, 1].astype(F32) * qkv_recv[j, 2].astype(F32)
 
@@ -349,13 +351,15 @@
         copy.start()
 
     forwards = []
-    for i, peer in enumerate(line_peers):
+
+    def forward_weights(i):
         w_copies[i].wait()
         source = lax.rem(me_c + n_ctx - 2 * (i + 1), n_ctx)
         copy = remote(wbuf.at[source], wbuf.at[source], w_ss.at[half + i], w_rs.at[half + i], ctx=partner)
         copy.start()
         forwards.append(copy)
 
+    forward_weights(0)
     for copy in b_copies:
         copy.wait()
     for k in range(n_ctx):
@@ -372,7 +376,7 @@
 
     line = me_c // 2
     y_copies = {}
-    for h in range(2):
+    for h in range(PARTS):
         for s in list(range(1, half)) + [0]:
             k = 2 * lax.rem(line + s, half) + 1 - side
             weight_block(k, h)
@@ -381,23 +385,15 @@
             )
             copy.start()
             y_copies[h, s] = copy
+        if h + 1 < half - 1:
+            forward_weights(h + 1)
 
     def own_blocks(z, carry):
-        for h in range(2):
+        for h in range(PARTS):
             weight_block(2 * z + side, h)
         return carry
 
     lax.fori_loop(0, half, own_blocks, 0)
-
-    own_w.wait()
-    w_copies[half - 1].wait()
-    for copy in forwards:
-        copy.wait()
-    gg_acc[...] = jnp.zeros_like(gg_acc)
-
-    def terms(k, carry):
-        gg_acc[...] += dot_nt(wbuf[k], gcols[k])
-        return carry
 
     z_copies = {}
 
@@ -432,6 +428,17 @@
             copy.start()
         return copies
 
+    pass_on(0)
+    own_w.wait()
+    w_copies[half - 1].wait()
+    for copy in forwards:
+        copy.wait()
+    gg_acc[...] = jnp.zeros_like(gg_acc)
+
+    def terms(k, carry):
+        gg_acc[...] += dot_nt(wbuf[k], gcols[k])
+        return carry
+
     lax.fori_loop(0, n_ctx, terms, 0)
     gg_send[...] = gg_acc[...].astype(BF16)
     c_copies = [
@@ -441,7 +448,7 @@
     for copy in c_copies:
         copy.start()
     gg_recv[me_d] = gg_send[:, rows(me_d, LANES)]
-    pass_on(0)
+    pass_on(1)
 
     for copy in c_copies:
         copy.wait()
@@ -456,7 +463,9 @@
     for copy in t_copies:
         copy.start()
     ggt_recv[me_c] = ggt_send[rows(me_c, mine), :]
-    pass_on(1)
+    pass_on(2)
+    f_copies = finish(0)
+    pass_on(3)
 
     for copy in t_copies:
         copy.wait()
@@ -501,8 +510,9 @@
         red[c, order:, :] = (timed - lane * plain) * grown
         return carry
 
+    f_copies += finish(1)
     lax.fori_loop(0, mine, lags, 0, unroll=4)
-    f_copies = finish(0)
+    f_copies += finish(2)
     sums = jnp.sum(red[...], axis=2)
     sums = jnp.concatenate([sums, rest], axis=1) + far_sums
     red_send[...] = jnp.where(column < order, sums, -pltpu.roll(weight_rows, order, 1) * sums)
@@ -514,7 +524,7 @@
         copy.start()
     red_recv[me_d] = red_send[...]
     lax.fori_loop(0, mine, backward, 0, unroll=8)
-    f_copies += finish(1)
+    f_copies += finish(3)
     for j in range(n_ctx):
         part = slice(j * mine, (j + 1) * mine)
         at = slice(j * LANES, (j + 1) * LANES)
@@ -582,7 +592,7 @@
         pltpu.VMEM((n_dp, mine, LANES), F32),
     ]
     scratch += twice(n_c) + twice(n_d, n_ctx) + twice(n_c) + twice(n_c) + twice(n_d) + twice(n_d)
-    scratch += twice(n_c) + twice(2, half) + twice(2, half - 1) + twice(2, n_d) + twice(n_d) + [sem((n_ctx + 1,))]
+    scratch += twice(n_c) + twice(PARTS, half) + twice(PARTS, half - 1) + twice(PARTS, n_d) + twice(n_d) + [sem((n_ctx + 1,))]
     blocks = jax.ShapeDtypeStruct((mine, n_ctx * LANES), BF16)
     params = jax.ShapeDtypeStruct((order, mine), F32)
     gq, gk, gv, dw, par_res, par_dec = pl.pallas_call(

time: 118 us -> 117 us (level)
  no operation moved by 1% of the time
where the time goes in v2:
time: 117 us; the launch traced here: 116 us
  Pallas kernels  110 us (94%)
  local copies, waits for them, and re-layouts  3.18 us (3%)
  other arithmetic  2.86 us (2%)
    pallas_call x1, Pallas kernels, fused_body(): pl.pallas_call(functools.partial(fused_kernel, n_dp, n_ctx), out_shape=(b...  110 us
    unnamed x15, local copies, waits for them, and re-layouts  3.18 us
    convert_element_type x1, other arithmetic, fused_body(): dw.astype(F32)  2.86 us

profile of v2, /device:TPU:0, one launch (start us, length us, event | category | flops | bytes accessed | tf_op | source)
XLA Modules:
  0.0 116.3 jit_solution(12724815276505109608)
XLA Ops:
  0.6 109.5 %shard_map.118 = (bf16[64,1024]{1,0:T(8,128)(2,1)}, bf16[64,1024]{1,0:T(8,128)(2,1)}, bf16[64,1024]{1,0:T(8,128)(2,1)}, bf16[512,1024]{1,0:T(8,128)(2,1)}, f32[16,64]{1,0:T(8,128)}, /*index=5*/f32[16,64]{1,0:T(8,128)}) custom-call(bf16[1,128,512]{2,1,0:T(8,128)(2,1)} %q_ref.1, bf16[1,128,512]{2,1,0:T(8,128)(2,1)} %k_ref.1, bf16[1,128,512]{2,1,0:T(8,128)(2,1)} %v_ref.1, ...), custom_call_target="tpu_custom_call" | custom-call | flops 6000000000 | bytes 8388608 | tf_op jit(solution)/shard_map/pallas_call | solution.py:598
  110.2 0.0 copy-start.2
  110.2 0.0 copy-start.1
  110.2 0.0 copy-start
  110.2 0.0 copy-start.4
  110.2 0.0 copy-start.3
  110.2 2.9 %convert_element_type.3 = f32[512,1024]{1,0:T(8,128)} convert(bf16[512,1024]{1,0:T(8,128)(2,1)} %get-tuple-element.15) | non-fusion elementwise | flops 524288 | bytes 3145728 | tf_op jit(solution)/shard_map/convert_element_type | solution.py:622
  113.1 0.0 copy-done.2
  113.1 0.7 copy.18
  113.7 0.0 copy-done.1
  113.7 0.7 copy.19
  114.4 0.0 copy-done
  114.4 0.7 copy.20
  115.1 0.0 copy-done.4
  115.1 0.6 copy.21
  115.7 0.0 copy-done.3
  115.7 0.6 copy.22
Async XLA Ops:
  110.2 2.9 %copy-start.2 = (bf16[64,1024]{1,0:T(8,128)(2,1)S(1)}, bf16[64,1024]{1,0:T(8,128)(2,1)}, u32[]{:S(2)}) copy-start(bf16[64,1024]{1,0:T(8,128)(2,1)} %get-tuple-element.12) | copy-start | bytes 393220
  110.2 3.6 %copy-start.1 = (bf16[64,1024]{1,0:T(8,128)(2,1)S(1)}, bf16[64,1024]{1,0:T(8,128)(2,1)}, u32[]{:S(2)}) copy-start(bf16[64,1024]{1,0:T(8,128)(2,1)} %get-tuple-element.13) | copy-start | bytes 393220
  110.2 4.2 %copy-start = (bf16[64,1024]{1,0:T(8,128)(2,1)S(1)}, bf16[64,1024]{1,0:T(8,128)(2,1)}, u32[]{:S(2)}) copy-start(bf16[64,1024]{1,0:T(8,128)(2,1)} %get-tuple-element.14) | copy-start | bytes 393220
  110.2 4.9 %copy-start.4 = (f32[16,64]{1,0:T(8,128)S(1)}, f32[16,64]{1,0:T(8,128)}, u32[]{:S(2)}) copy-start(f32[16,64]{1,0:T(8,128)} %get-tuple-element.16) | copy-start | bytes 12292
  110.2 5.4 %copy-start.3 = (f32[16,64]{1,0:T(8,128)S(1)}, f32[16,64]{1,0:T(8,128)}, u32[]{:S(2)}) copy-start(f32[16,64]{1,0:T(8,128)} %get-tuple-element.17) | copy-start | bytes 12292

commit v3 on v2

--- a/solution.py
+++ b/solution.py
@@ -203,6 +203,9 @@
     partner = me_c + 1 - 2 * side
     ctx_peers = [lax.rem(me_c + s, n_ctx) for s in range(1, n_ctx)]
     dp_peers = [lax.rem(me_d + s, n_dp) for s in range(1, n_dp)]
+    sibling = me_d + 1 - 2 * lax.rem(me_d, 2)
+    far_peers = [lax.rem(me_d + 2 * s, n_dp) for s in range(1, n_dp // 2)]
+    far_sources = [lax.rem(me_d + n_dp - 2 * s, n_dp) for s in range(1, n_dp // 2)]
     line_peers = [lax.rem(me_c + 2 * s, n_ctx) for s in range(1, half)]
 
     def remote(src, dst, ss, rs, **to):
@@ -302,6 +305,13 @@
         copy.wait()
     for copy in w_copies[: half - 1]:
         copy.start()
+    w_copies[half - 1].wait()
+    for i, peer in enumerate(line_peers):
+        copy = remote(
+            wbuf.at[partner], wbuf.at[partner], w_ss.at[half + i], w_rs.at[half + i], ctx=peer
+        )
+        copy.start()
+        w_copies.append(copy)
     for j in range(n_ctx):
         prod[j * mine : (j + 1) * mine, :] = qkv_recv[j, 1].astype(F32) * qkv_recv[j, 2].astype(F32)
 
@@ -345,22 +355,20 @@
             gat_all.at[:, rows(me_d, LANES)], gat_all.at[:, rows(me_d, LANES)],
             b_ss.at[i], b_rs.at[i], dp=peer,
         )
-        for i, peer in enumerate(dp_peers)
+        for i, peer in enumerate(far_peers + [sibling])
     ]
     for copy in b_copies:
         copy.start()
 
-    forwards = []
-
-    def forward_weights(i):
-        w_copies[i].wait()
-        source = lax.rem(me_c + n_ctx - 2 * (i + 1), n_ctx)
-        copy = remote(wbuf.at[source], wbuf.at[source], w_ss.at[half + i], w_rs.at[half + i], ctx=partner)
-        copy.start()
-        forwards.append(copy)
-
-    forward_weights(0)
-    for copy in b_copies:
+    for i, source in enumerate(far_sources):
+        b_copies[i].wait()
+        copy = remote(
+            gat_all.at[:, rows(source, LANES)], gat_all.at[:, rows(source, LANES)],
+            b_ss.at[n_dp // 2 + i], b_rs.at[n_dp // 2 + i], dp=sibling,
+        )
+        copy.start()
+        b_copies.append(copy)
+    for copy in b_copies[n_dp // 2 - 1 :]:
         copy.wait()
     for k in range(n_ctx):
         for i, peer in enumerate(dp_peers):
@@ -385,8 +393,6 @@
             )
             copy.start()
             y_copies[h, s] = copy
-        if h + 1 < half - 1:
-            forward_weights(h + 1)
 
     def own_blocks(z, carry):
         for h in range(PARTS):
@@ -422,16 +428,26 @@
                 dwf.at[part, rows(me_d, width)], dwf.at[part, rows(me_d, width)],
                 f_ss.at[h, i], f_rs.at[h, i], dp=peer,
             )
-            for i, peer in enumerate(dp_peers)
+            for i, peer in enumerate(far_peers + [sibling])
         ]
         for copy in copies:
             copy.start()
         return copies
 
+    def share(h):
+        part = part_of(h)
+        for i, source in enumerate(far_sources):
+            f_copies[h][i].wait()
+            copy = remote(
+                dwf.at[part, rows(source, width)], dwf.at[part, rows(source, width)],
+                f_ss.at[h, n_dp // 2 + i], f_rs.at[h, n_dp // 2 + i], dp=sibling,
+            )
+            copy.start()
+            f_copies[h].append(copy)
+
     pass_on(0)
     own_w.wait()
-    w_copies[half - 1].wait()
-    for copy in forwards:
+    for copy in w_copies[: half - 1] + w_copies[half:]:
         copy.wait()
     gg_acc[...] = jnp.zeros_like(gg_acc)
 
@@ -464,7 +480,7 @@
         copy.start()
     ggt_recv[me_c] = ggt_send[rows(me_c, mine), :]
     pass_on(2)
-    f_copies = finish(0)
+    f_copies = [finish(0)]
     pass_on(3)
 
     for copy in t_copies:
@@ -510,9 +526,11 @@
         red[c, order:, :] = (timed - lane * plain) * grown
         return carry
 
-    f_copies += finish(1)
+    f_copies.append(finish(1))
+    share(0)
     lax.fori_loop(0, mine, lags, 0, unroll=4)
-    f_copies += finish(2)
+    f_copies.append(finish(2))
+    share(1)
     sums = jnp.sum(red[...], axis=2)
     sums = jnp.concatenate([sums, rest], axis=1) + far_sums
     red_send[...] = jnp.where(column < order, sums, -pltpu.roll(weight_rows, order, 1) * sums)
@@ -524,12 +542,14 @@
         copy.start()
     red_recv[me_d] = red_send[...]
     lax.fori_loop(0, mine, backward, 0, unroll=8)
-    f_copies += finish(3)
+    f_copies.append(finish(3))
+    share(2)
     for j in range(n_ctx):
         part = slice(j * mine, (j + 1) * mine)
         at = slice(j * LANES, (j + 1) * LANES)
         gk_ref[:, at] = (gprod[part, :] * qkv_recv[j, 2].astype(F32)).astype(BF16)
         gv_ref[:, at] = (gprod[part, :] * qkv_recv[j, 1].astype(F32)).astype(BF16)
+    share(3)
     for copy in r_copies:
         copy.wait()
     total = red_recv[0]
@@ -538,8 +558,9 @@
     turned = total.T
     par_res_ref[...] = turned[0:order, :]
     par_dec_ref[...] = turned[order : 2 * order, :]
-    for copy in f_copies:
-        copy.wait()
+    for copies in f_copies:
+        for copy in copies[n_dp // 2 - 1 :]:
+            copy.wait()
     dw_ref[...] = dwf[...]
 
 
@@ -627,7 +648,8 @@
     chans, columns = out_weight.shape
     return (
         n_ctx == 8
-        and n_dp >= 2
+        and n_dp >= 4
+        and n_dp % 2 == 0
         and queries.shape[0] == n_dp
         and queries.shape[1] == n_ctx * LANES
         and chans % (n_ctx * 16) == 0

time: 117 us -> 124 us (1.060)
  Pallas kernels: 110 us -> 117 us
    pallas_call x1, Pallas kernels: 110 us -> 117 us  [fused_body(): pl.pallas_call(functools.partial(fused_kernel, n_dp, n_ctx), out_shape=(b...]
where the time goes in v3:
time: 124 us
  Pallas kernels  117 us (94%)
  local copies, waits for them, and re-layouts  3.18 us (3%)
  other arithmetic  2.86 us (2%)
    pallas_call x1, Pallas kernels, fused_body(): pl.pallas_call(functools.partial(fused_kernel, n_dp, n_ctx), out_shape=(b...  117 us
    unnamed x15, local copies, waits for them, and re-layouts  3.18 us
    convert_element_type x1, other arithmetic, fused_body(): dw.astype(F32)  2.86 us

profile of v3, /device:TPU:0, one launch (start us, length us, event | category | flops | bytes accessed | tf_op | source)
XLA Modules:
  0.0 123.8 jit_solution(497878106370686625)
XLA Ops:
  0.6 117.1 %shard_map.118 = (bf16[64,1024]{1,0:T(8,128)(2,1)}, bf16[64,1024]{1,0:T(8,128)(2,1)}, bf16[64,1024]{1,0:T(8,128)(2,1)}, bf16[512,1024]{1,0:T(8,128)(2,1)}, f32[16,64]{1,0:T(8,128)}, /*index=5*/f32[16,64]{1,0:T(8,128)}) custom-call(bf16[1,128,512]{2,1,0:T(8,128)(2,1)} %q_ref.1, bf16[1,128,512]{2,1,0:T(8,128)(2,1)} %k_ref.1, bf16[1,128,512]{2,1,0:T(8,128)(2,1)} %v_ref.1, ...), custom_call_target="tpu_custom_call" | custom-call | flops 6000000000 | bytes 8388608 | tf_op jit(solution)/shard_map/pallas_call | solution.py:619
  117.7 0.0 copy-start.2
  117.7 0.0 copy-start.1
  117.7 0.0 copy-start
  117.7 0.0 copy-start.4
  117.8 0.0 copy-start.3
  117.8 2.9 %convert_element_type.3 = f32[512,1024]{1,0:T(8,128)} convert(bf16[512,1024]{1,0:T(8,128)(2,1)} %get-tuple-element.15) | non-fusion elementwise | flops 524288 | bytes 3145728 | tf_op jit(solution)/shard_map/convert_element_type | solution.py:643
  120.6 0.0 copy-done.2
  120.6 0.7 copy.18
  121.3 0.0 copy-done.1
  121.3 0.7 copy.19
  121.9 0.0 copy-done
  121.9 0.7 copy.20
  122.6 0.0 copy-done.4
  122.6 0.6 copy.21
  123.2 0.0 copy-done.3
  123.2 0.6 copy.22
Async XLA Ops:
  117.7 2.9 %copy-start.2 = (bf16[64,1024]{1,0:T(8,128)(2,1)S(1)}, bf16[64,1024]{1,0:T(8,128)(2,1)}, u32[]{:S(2)}) copy-start(bf16[64,1024]{1,0:T(8,128)(2,1)} %get-tuple-element.12) | copy-start | bytes 393220
  117.7 3.6 %copy-start.1 = (bf16[64,1024]{1,0:T(8,128)(2,1)S(1)}, bf16[64,1024]{1,0:T(8,128)(2,1)}, u32[]{:S(2)}) copy-start(bf16[64,1024]{1,0:T(8,128)(2,1)} %get-tuple-element.13) | copy-start | bytes 393220
  117.7 4.2 %copy-start = (bf16[64,1024]{1,0:T(8,128)(2,1)S(1)}, bf16[64,1024]{1,0:T(8,128)(2,1)}, u32[]{:S(2)}) copy-start(bf16[64,1024]{1,0:T(8,128)(2,1)} %get-tuple-element.14) | copy-start | bytes 393220
  117.7 4.9 %copy-start.4 = (f32[16,64]{1,0:T(8,128)S(1)}, f32[16,64]{1,0:T(8,128)}, u32[]{:S(2)}) copy-start(f32[16,64]{1,0:T(8,128)} %get-tuple-element.16) | copy-start | bytes 12292
  117.8 5.4 %copy-start.3 = (f32[16,64]{1,0:T(8,128)S(1)}, f32[16,64]{1,0:T(8,128)}, u32[]{:S(2)}) copy-start(f32[16,64]{1,0:T(8,128)} %get-tuple-element.17) | copy-start | bytes 12292

commit v4 on v3

--- a/solution.py
+++ b/solution.py
@@ -305,13 +305,6 @@
         copy.wait()
     for copy in w_copies[: half - 1]:
         copy.start()
-    w_copies[half - 1].wait()
-    for i, peer in enumerate(line_peers):
-        copy = remote(
-            wbuf.at[partner], wbuf.at[partner], w_ss.at[half + i], w_rs.at[half + i], ctx=peer
-        )
-        copy.start()
-        w_copies.append(copy)
     for j in range(n_ctx):
         prod[j * mine : (j + 1) * mine, :] = qkv_recv[j, 1].astype(F32) * qkv_recv[j, 2].astype(F32)
 
@@ -360,6 +353,16 @@
     for copy in b_copies:
         copy.start()
 
+    forwards = []
+
+    def forward_weights(i):
+        w_copies[i].wait()
+        source = lax.rem(me_c + n_ctx - 2 * (i + 1), n_ctx)
+        copy = remote(wbuf.at[source], wbuf.at[source], w_ss.at[half + i], w_rs.at[half + i], ctx=partner)
+        copy.start()
+        forwards.append(copy)
+
+    forward_weights(0)
     for i, source in enumerate(far_sources):
         b_copies[i].wait()
         copy = remote(
@@ -393,6 +396,8 @@
             )
             copy.start()
             y_copies[h, s] = copy
+        if h + 1 < half - 1:
+            forward_weights(h + 1)
 
     def own_blocks(z, carry):
         for h in range(PARTS):
@@ -447,7 +452,8 @@
 
     pass_on(0)
     own_w.wait()
-    for copy in w_copies[: half - 1] + w_copies[half:]:
+    w_copies[half - 1].wait()
+    for copy in forwards:
         copy.wait()
     gg_acc[...] = jnp.zeros_like(gg_acc)
 

time: 124 us -> 116 us (0.935)
  Pallas kernels: 117 us -> 109 us
    pallas_call x1, Pallas kernels: 117 us -> 109 us  [fused_body(): pl.pallas_call(functools.partial(fused_kernel, n_dp, n_ctx), out_shape=(b...]
where the time goes in v4:
time: 116 us
  Pallas kernels  109 us (94%)
  local copies, waits for them, and re-layouts  3.18 us (3%)
  other arithmetic  2.86 us (2%)
    pallas_call x1, Pallas kernels, fused_body(): pl.pallas_call(functools.partial(fused_kernel, n_dp, n_ctx), out_shape=(b...  109 us
    unnamed x15, local copies, waits for them, and re-layouts  3.18 us
    convert_element_type x1, other arithmetic, fused_body(): dw.astype(F32)  2.86 us

profile of v4, /device:TPU:0, one launch (start us, length us, event | category | flops | bytes accessed | tf_op | source)
XLA Modules:
  0.0 116.1 jit_solution(7658349271368967311)
XLA Ops:
  0.6 109.4 %shard_map.118 = (bf16[64,1024]{1,0:T(8,128)(2,1)}, bf16[64,1024]{1,0:T(8,128)(2,1)}, bf16[64,1024]{1,0:T(8,128)(2,1)}, bf16[512,1024]{1,0:T(8,128)(2,1)}, f32[16,64]{1,0:T(8,128)}, /*index=5*/f32[16,64]{1,0:T(8,128)}) custom-call(bf16[1,128,512]{2,1,0:T(8,128)(2,1)} %q_ref.1, bf16[1,128,512]{2,1,0:T(8,128)(2,1)} %k_ref.1, bf16[1,128,512]{2,1,0:T(8,128)(2,1)} %v_ref.1, ...), custom_call_target="tpu_custom_call" | custom-call | flops 6000000000 | bytes 8388608 | tf_op jit(solution)/shard_map/pallas_call | solution.py:625
  110.0 0.0 copy-start.2
  110.0 0.0 copy-start.1
  110.0 0.0 copy-start
  110.0 0.0 copy-start.4
  110.0 0.0 copy-start.3
  110.0 2.9 %convert_element_type.3 = f32[512,1024]{1,0:T(8,128)} convert(bf16[512,1024]{1,0:T(8,128)(2,1)} %get-tuple-element.15) | non-fusion elementwise | flops 524288 | bytes 3145728 | tf_op jit(solution)/shard_map/convert_element_type | solution.py:649
  112.9 0.0 copy-done.2
  112.9 0.7 copy.18
  113.6 0.0 copy-done.1
  113.6 0.7 copy.19
  114.2 0.0 copy-done
  114.2 0.7 copy.20
  114.9 0.0 copy-done.4
  114.9 0.6 copy.21
  115.5 0.0 copy-done.3
  115.5 0.6 copy.22
Async XLA Ops:
  110.0 2.9 %copy-start.2 = (bf16[64,1024]{1,0:T(8,128)(2,1)S(1)}, bf16[64,1024]{1,0:T(8,128)(2,1)}, u32[]{:S(2)}) copy-start(bf16[64,1024]{1,0:T(8,128)(2,1)} %get-tuple-element.12) | copy-start | bytes 393220
  110.0 3.6 %copy-start.1 = (bf16[64,1024]{1,0:T(8,128)(2,1)S(1)}, bf16[64,1024]{1,0:T(8,128)(2,1)}, u32[]{:S(2)}) copy-start(bf16[64,1024]{1,0:T(8,128)(2,1)} %get-tuple-element.13) | copy-start | bytes 393220
  110.0 4.2 %copy-start = (bf16[64,1024]{1,0:T(8,128)(2,1)S(1)}, bf16[64,1024]{1,0:T(8,128)(2,1)}, u32[]{:S(2)}) copy-start(bf16[64,1024]{1,0:T(8,128)(2,1)} %get-tuple-element.14) | copy-start | bytes 393220
  110.0 4.9 %copy-start.4 = (f32[16,64]{1,0:T(8,128)S(1)}, f32[16,64]{1,0:T(8,128)}, u32[]{:S(2)}) copy-start(f32[16,64]{1,0:T(8,128)} %get-tuple-element.16) | copy-start | bytes 12292
  110.0 5.4 %copy-start.3 = (f32[16,64]{1,0:T(8,128)S(1)}, f32[16,64]{1,0:T(8,128)}, u32[]{:S(2)}) copy-start(f32[16,64]{1,0:T(8,128)} %get-tuple-element.17) | copy-start | bytes 12292
